TPU v7x, 256 devices: a whole 4x4x8 slice. The times are simulated.
256 devices in a mesh: seq: 64 (over z, y, core), ch: 4 (over x).
Axes of the slice: x: 4, y: 4, z: 8, core: 2. Of those that a mesh axis runs over, the one named last changes fastest.
Arguments:
- value_in: bfloat16 [4, 512, 8192], P('ch', None, 'seq'), may hold values from -6 to 6
- gate_in: bfloat16 [4, 512, 8192], P('ch', None, 'seq'), may hold values from -6 to 6
- grad_out: bfloat16 [4, 512, 8192], P('ch', None, 'seq'), may hold values from -6 to 6
- filters: float32 [512, 8192], P('seq'), may hold values from -2 to 2
- genome_lengths: int32 [4], replicated, may hold values from 512 to 4096, as said below
Outputs:
- gated_out: bfloat16 [4, 512, 8192], P('ch', None, 'seq')
- grad_value: bfloat16 [4, 512, 8192], P('ch', None, 'seq')
- grad_gate: bfloat16 [4, 512, 8192], P('ch', None, 'seq')
- grad_filters: float32 [512, 8192], P('seq', 'ch')
Inputs may be any that keep to these rules, and one draw needn't show every extreme that they name: `genome_lengths`: the lengths are multiples of 512, sum to 8192, and one of them is exactly 4096.
All inputs are finite; a program needn't handle non-finite values.
Results may differ from a plain program's by a relative error of at most 0.012.
Values may be sent and summed in bfloat16 or wider, within the bound.
A program may use at most 128 MiB of HBM per device.

v0:
```python
import functools

import jax
import jax.numpy as jnp
from jax import lax
from jax.experimental import pallas as pl
from jax.experimental.pallas import tpu as pltpu
from jax.sharding import PartitionSpec as P

MESH = pl.DeviceIdType.MESH
F32 = jnp.float32
BF16 = jnp.bfloat16

PEERS = 64
NFL = 8
TOK = 128
ROWS = 32
LAGS = 16
SPAN = 4096


def anti_identity(n, dtype):
    row = lax.broadcasted_iota(jnp.int32, (n, n), 0)
    col = lax.broadcasted_iota(jnp.int32, (n, n), 1)
    return (row + col == n - 1).astype(dtype)


def partner(k, seq):
    z, y, c = seq >> 3, (seq >> 1) & 3, seq & 1
    dz, dy, dc = (3 * k) & 7, ((k >> 3) + k) & 3, k >> 5
    return (((((z + dz) & 7) << 2) + ((y + dy) & 3)) << 1) + (c ^ dc)


def kernel(
    lengths, value, gate, cot, filt,
    gated, grad_value, grad_gate, grad_filters,
    send1, recv1, send2, recv2, unpacked, result, xpad, gpad, toep, xcat, diag, gsend, grecv,
    ssem1, rsem1, ssem2, rsem2, gssem, grsem,
):
    seq = lax.axis_index("seq")
    ch = lax.axis_index("ch")

    barrier = pltpu.get_barrier_semaphore()

    def greet(k, carry):
        pl.semaphore_signal(barrier, inc=1, device_id=(partner(k, seq), ch), device_id_type=MESH)
        return carry

    lax.fori_loop(1, PEERS, greet, 0, unroll=7)
    for step in range(1, 4):
        pl.semaphore_signal(barrier, inc=1, device_id=(seq, (ch + step) & 3), device_id_type=MESH)

    flip = anti_identity(TOK, BF16)
    grad_conv = (cot[...].astype(F32) * gate[...].astype(F32)).astype(BF16)
    reverse = jnp.dot(grad_conv, flip, preferred_element_type=F32)
    both = jnp.concatenate(
        [value[...].astype(F32).reshape(PEERS, NFL, TOK), reverse.reshape(PEERS, NFL, TOK)], axis=1
    )
    send1[...] = both.astype(BF16)

    pl.semaphore_wait(barrier, PEERS + 2)

    def share1(k, carry):
        to = partner(k, seq)
        pltpu.make_async_remote_copy(
            src_ref=send1.at[to], dst_ref=recv1.at[seq], send_sem=ssem1, recv_sem=rsem1,
            device_id=(to, ch), device_id_type=MESH,
        ).start()
        return carry

    lax.fori_loop(1, PEERS, share1, 0, unroll=7)
    recv1[pl.ds(seq, 1)] = send1[pl.ds(seq, 1)]

    lane_zero = jnp.zeros((8, TOK), F32)
    for f in range(NFL):
        row = jnp.broadcast_to(filt[f : f + 1, 0:SPAN], (8, SPAN))
        row = jnp.concatenate([lane_zero, row], axis=1)
        for q in range(0, 16, 2):
            upper = pltpu.roll(row, 8 * q, 1, stride=1, stride_axis=0)
            lower = pltpu.roll(row, 8 * q + 8, 1, stride=1, stride_axis=0)
            toep[f, 8 * q : 8 * q + 16, :] = jnp.concatenate([upper, lower], axis=0).astype(BF16)
        toep[f, :, 0:TOK] = jnp.zeros((TOK, TOK), BF16)

    block = lax.broadcasted_iota(jnp.int32, (ROWS, TOK), 0)
    first = jnp.zeros((ROWS, TOK), jnp.int32)
    last = jnp.full((ROWS, TOK), ROWS, jnp.int32)
    edge = jnp.int32(0)
    for genome in range(4):
        first = jnp.where(block >= edge, edge, first)
        edge = edge + (lengths[genome] >> 8)
        last = jnp.minimum(last, jnp.where(block < edge, edge, ROWS))
    before = block - first
    after = last - 1 - block

    pltpu.make_async_copy(
        send1.at[pl.ds(0, PEERS - 1)], send1.at[pl.ds(0, PEERS - 1)], ssem1
    ).wait()
    pltpu.make_async_copy(
        recv1.at[pl.ds(0, PEERS - 1)], recv1.at[pl.ds(0, PEERS - 1)], rsem1
    ).wait()

    unpacked[...] = recv1[...].astype(F32).reshape(PEERS * 16, TOK)
    xpad[:, 0:LAGS, :] = jnp.zeros((NFL, LAGS, 256), F32)
    gpad[:, ROWS : ROWS + LAGS, :] = jnp.zeros((NFL, LAGS, 256), F32)
    flip2 = anti_identity(256, BF16)
    for f in range(NFL):
        xpad[f, LAGS : LAGS + ROWS, 0:TOK] = unpacked[pl.ds(f, ROWS, stride=32), :]
        xpad[f, LAGS : LAGS + ROWS, TOK:256] = unpacked[pl.ds(16 + f, ROWS, stride=32), :]
        gpad[f, 0:ROWS, TOK:256] = unpacked[pl.ds(8 + f, ROWS, stride=32), :]
        gpad[f, 0:ROWS, 0:TOK] = unpacked[pl.ds(24 + f, ROWS, stride=32), :]
        left, right = [], []
        for lag in range(LAGS):
            back = xpad[f, LAGS - lag : LAGS - lag + ROWS, :]
            ahead = gpad[f, lag : lag + ROWS, :]
            keep_x = jnp.concatenate([before >= lag] * 2, axis=1)
            keep_g = jnp.concatenate([after >= lag] * 2, axis=1)
            piece = jnp.concatenate(
                [jnp.where(keep_x, back, 0.0), jnp.where(keep_g, ahead, 0.0)], axis=0
            ).astype(BF16)
            xcat[f, :, 256 * lag : 256 * lag + 256] = piece[0:ROWS]
            left.append(piece)
            right.append(toep[f, :, 256 * lag + 128 : 256 * lag + 384])
            right.append(toep[f, :, 256 * lag : 256 * lag + 256])
        out = jnp.dot(
            jnp.concatenate(left, axis=1), jnp.concatenate(right, axis=0), preferred_element_type=F32
        )
        back = jnp.dot(out[ROWS:].astype(BF16), flip2, preferred_element_type=F32)
        result[pl.ds(f, ROWS, stride=32), :] = out[0:ROWS, 0:TOK]
        result[pl.ds(16 + f, ROWS, stride=32), :] = out[0:ROWS, TOK:256]
        result[pl.ds(8 + f, ROWS, stride=32), :] = back[:, 0:TOK]
        result[pl.ds(24 + f, ROWS, stride=32), :] = back[:, TOK:256]
    send2[...] = result[...].reshape(PEERS, 16, TOK).astype(BF16)

    def share2(k, carry):
        to = partner(k, seq)
        pltpu.make_async_remote_copy(
            src_ref=send2.at[to], dst_ref=recv2.at[seq], send_sem=ssem2, recv_sem=rsem2,
            device_id=(to, ch), device_id_type=MESH,
        ).start()
        return carry

    lax.fori_loop(1, PEERS, share2, 0, unroll=7)
    recv2[pl.ds(seq, 1)] = send2[pl.ds(seq, 1)]

    zero_tile = jnp.zeros((ROWS, TOK), BF16)
    for f in range(NFL):
        lhs = jnp.concatenate([gpad[f, 0:ROWS, TOK:256], gpad[f, 0:ROWS, 0:TOK]], axis=0).astype(BF16)
        tiles = []
        for d in range(2 * LAGS - 1, -1, -1):
            lag = d // 2
            if d % 2:
                if lag + 1 < LAGS:
                    even = xcat[f, :, 256 * lag + 384 : 256 * lag + 512]
                else:
                    even = zero_tile
                odd = xcat[f, :, 256 * lag : 256 * lag + 128]
            else:
                even = xcat[f, :, 256 * lag : 256 * lag + 128]
                odd = xcat[f, :, 256 * lag + 128 : 256 * lag + 256]
            tiles.append(jnp.concatenate([even, odd], axis=0))
        cross = lax.dot_general(
            lhs, jnp.concatenate(tiles, axis=1), (((0,), (0,)), ((), ())), preferred_element_type=F32
        )
        cross = jnp.concatenate([cross, jnp.zeros((TOK, TOK), F32)], axis=1)
        half = TOK // 2
        while half >= 8:
            cross = cross[0:half] + pltpu.roll(cross[half : 2 * half], half, 1)
            half //= 2
        cross = pltpu.roll(cross, 0, 1, stride=1, stride_axis=0)
        for tile in range(32):
            diag[8 * tile : 8 * tile + 8, :] = cross[:, TOK * tile : TOK * tile + TOK]
        total = diag[pl.ds(0, 32, stride=8), :]
        for j in range(1, 8):
            total = total + diag[pl.ds(j, 32, stride=8), :]
        total = jnp.dot(total, anti_identity(TOK, F32), precision=lax.Precision.HIGHEST, preferred_element_type=F32)
        gsend[0, 16 * f : 16 * f + 16, :] = total[16:32]
        gsend[1, 16 * f : 16 * f + 16, :] = total[0:16]

    for part in range(2):
        copy = pltpu.make_async_remote_copy(
            src_ref=gsend.at[part], dst_ref=grecv.at[ch], send_sem=gssem.at[part], recv_sem=grsem.at[ch],
            device_id=(seq, jnp.int32(part)), device_id_type=MESH,
        )
        pl.when(ch != part)(copy.start)

        @pl.when(ch == part)
        def _():
            grecv[pl.ds(ch, 1)] = gsend[part : part + 1]

    pltpu.make_async_copy(
        send2.at[pl.ds(0, PEERS - 1)], send2.at[pl.ds(0, PEERS - 1)], ssem2
    ).wait()
    pltpu.make_async_copy(
        recv2.at[pl.ds(0, PEERS - 1)], recv2.at[pl.ds(0, PEERS - 1)], rsem2
    ).wait()

    arrived = recv2[...].astype(F32)
    conv = arrived[:, 0:8].reshape(PEERS * NFL, TOK)
    gated[...] = (gate[...].astype(F32) * conv).astype(BF16)
    grad_gate[...] = (cot[...].astype(F32) * conv).astype(BF16)
    grad_value[...] = arrived[:, 8:16].reshape(PEERS * NFL, TOK).astype(BF16)

    for part in range(2):
        @pl.when(ch != part)
        def _():
            pltpu.make_async_copy(gsend.at[part], gsend.at[part], gssem.at[part]).wait()

    @pl.when(ch < 2)
    def _():
        for source in range(4):
            @pl.when(ch != source)
            def _():
                pltpu.make_async_copy(grecv.at[source], grecv.at[source], grsem.at[source]).wait()
        diag[0:128, :] = grecv[0] + grecv[1] + grecv[2] + grecv[3]
        for tile in range(16):
            grad_filters[:, TOK * (15 - tile) : TOK * (16 - tile)] = diag[pl.ds(tile, NFL, stride=16), :]

    @pl.when(ch >= 2)
    def _():
        grad_filters[...] = jnp.zeros((NFL, 2048), F32)


def per_device(value_in, gate_in, grad_out, filters, genome_lengths):
    shape = value_in.shape
    flat = (shape[1], shape[2])
    vmem = pl.BlockSpec(memory_space=pltpu.VMEM)
    messages = (PEERS, 16, TOK)
    outs = pl.pallas_call(
        kernel,
        out_shape=[jax.ShapeDtypeStruct(flat, BF16)] * 3 + [jax.ShapeDtypeStruct((NFL, 2048), F32)],
        in_specs=[
            pl.BlockSpec(memory_space=pltpu.SMEM), vmem, vmem, vmem,
            vmem,
        ],
        out_specs=[vmem] * 4,
        scratch_shapes=[
            pltpu.VMEM(messages, BF16), pltpu.VMEM(messages, BF16),
            pltpu.VMEM(messages, BF16), pltpu.VMEM(messages, BF16),
            pltpu.VMEM((PEERS * 16, TOK), F32), pltpu.VMEM((PEERS * 16, TOK), F32),
            pltpu.VMEM((NFL, ROWS + LAGS, 256), F32), pltpu.VMEM((NFL, ROWS + LAGS, 256), F32),
            pltpu.VMEM((NFL, TOK, SPAN + TOK), BF16),
            pltpu.VMEM((NFL, ROWS, SPAN), BF16),
            pltpu.VMEM((256, TOK), F32),
            pltpu.VMEM((2, 128, TOK), F32), pltpu.VMEM((4, 128, TOK), F32),
            pltpu.SemaphoreType.DMA, pltpu.SemaphoreType.DMA,
            pltpu.SemaphoreType.DMA, pltpu.SemaphoreType.DMA,
            pltpu.SemaphoreType.DMA((2,)), pltpu.SemaphoreType.DMA((4,)),
        ],
        compiler_params=pltpu.CompilerParams(
            collective_id=0, has_side_effects=True, vmem_limit_bytes=48 * 1024 * 1024
        ),
        name="hyena",
    )(genome_lengths, value_in.reshape(flat), gate_in.reshape(flat), grad_out.reshape(flat), filters)
    return (outs[0].reshape(shape), outs[1].reshape(shape), outs[2].reshape(shape), outs[3])


def solution(mesh):
    tokens = P("ch", None, "seq")
    return jax.shard_map(
        per_device,
        mesh=mesh,
        in_specs=(tokens, tokens, tokens, P("seq", None), P()),
        out_specs=(tokens, tokens, tokens, P("seq", "ch")),
        check_vma=False,
    )
```

profile of v0, /device:TPU:1, one launch (start us, length us, event | category | flops | bytes accessed | tf_op | source)
XLA Modules:
  0.0 51.9 jit_solution(9019147659506459212)
XLA Ops:
  0.6 0.0 copy-start.4
  0.6 0.6 %copy-done.4 = s32[4]{0:T(128)S(1)} copy-done((s32[4]{0:T(128)S(1)}, s32[4]{0:T(128)}, u32[]{:S(2)}) %copy-start.4) | copy-done | bytes 40
  1.3 0.0 copy-start
  1.3 0.9 %copy-done = f32[8,8192]{1,0:T(8,128)S(1)} copy-done((f32[8,8192]{1,0:T(8,128)S(1)}, f32[8,8192]{1,0:T(8,128)}, u32[]{:S(2)}) %copy-start) | copy-done | bytes 262168
  2.2 0.0 copy-start.1
  2.2 0.9 %copy-done.1 = bf16[1,512,128]{2,1,0:T(8,128)(2,1)S(1)} copy-done((bf16[1,512,128]{2,1,0:T(8,128)(2,1)S(1)}, bf16[1,512,128]{2,1,0:T(8,128)(2,1)}, u32[]{:S(2)}) %copy-start.1) | copy-done | bytes 131096
  3.1 0.0 copy-start.2
  3.1 0.9 %copy-done.2 = bf16[1,512,128]{2,1,0:T(8,128)(2,1)S(1)} copy-done((bf16[1,512,128]{2,1,0:T(8,128)(2,1)S(1)}, bf16[1,512,128]{2,1,0:T(8,128)(2,1)}, u32[]{:S(2)}) %copy-start.2) | copy-done | bytes 131096
  4.0 0.0 copy-start.3
  4.1 0.9 %copy-done.3 = bf16[1,512,128]{2,1,0:T(8,128)(2,1)S(1)} copy-done((bf16[1,512,128]{2,1,0:T(8,128)(2,1)S(1)}, bf16[1,512,128]{2,1,0:T(8,128)(2,1)}, u32[]{:S(2)}) %copy-start.3) | copy-done | bytes 131096
  5.0 44.4 %hyena.1 = (bf16[512,128]{1,0:T(8,128)(2,1)S(1)}, bf16[512,128]{1,0:T(8,128)(2,1)S(1)}, bf16[512,128]{1,0:T(8,128)(2,1)S(1)}, f32[8,2048]{1,0:T(8,128)S(1)}) custom-call(s32[4]{0:T(128)S(1)} %copy-done.4, bf16[512,128]{1,0:T(8,128)(2,1)S(1)} %bitcast.9, bf16[512,128]{1,0:T(8,128)(2,1)S(1)} %bitcast.10, bf16[512,128]{1,0:T(8,128)(2,1)S(1)} %bitcast.11, ...), custom_call_target="tpu_custom_call" | custom-call | tf_op jit(solution)/shard_map/hyena/pallas_call | solution.py:228
  49.3 0.7 %copy.13 = bf16[1,512,128]{2,1,0:T(8,128)(2,1)} copy(bf16[1,512,128]{2,1,0:T(8,128)(2,1)S(1)} %bitcast.8) | data formatting | bytes 262144
  50.0 0.7 %copy.14 = bf16[1,512,128]{2,1,0:T(8,128)(2,1)} copy(bf16[1,512,128]{2,1,0:T(8,128)(2,1)S(1)} %bitcast.7) | data formatting | bytes 262144
  50.6 0.7 %copy.15 = bf16[1,512,128]{2,1,0:T(8,128)(2,1)} copy(bf16[1,512,128]{2,1,0:T(8,128)(2,1)S(1)} %bitcast.6) | data formatting | bytes 262144
  51.3 0.6 %copy.16 = f32[8,2048]{1,0:T(8,128)} copy(f32[8,2048]{1,0:T(8,128)S(1)} %get-tuple-element.19) | data formatting | bytes 131072
Async XLA Ops:
  0.6 0.7 %copy-start.4 = (s32[4]{0:T(128)S(1)}, s32[4]{0:T(128)}, u32[]{:S(2)}) copy-start(s32[4]{0:T(128)} %lengths.1) | copy-start | bytes 52
  1.3 0.9 %copy-start = (f32[8,8192]{1,0:T(8,128)S(1)}, f32[8,8192]{1,0:T(8,128)}, u32[]{:S(2)}) copy-start(f32[8,8192]{1,0:T(8,128)} %filt.1) | copy-start | bytes 786436
  2.2 0.9 %copy-start.1 = (bf16[1,512,128]{2,1,0:T(8,128)(2,1)S(1)}, bf16[1,512,128]{2,1,0:T(8,128)(2,1)}, u32[]{:S(2)}) copy-start(bf16[1,512,128]{2,1,0:T(8,128)(2,1)} %param.5) | copy-start | bytes 393220
  3.1 0.9 %copy-start.2 = (bf16[1,512,128]{2,1,0:T(8,128)(2,1)S(1)}, bf16[1,512,128]{2,1,0:T(8,128)(2,1)}, u32[]{:S(2)}) copy-start(bf16[1,512,128]{2,1,0:T(8,128)(2,1)} %param.6) | copy-start | bytes 393220
  4.0 0.9 %copy-start.3 = (bf16[1,512,128]{2,1,0:T(8,128)(2,1)S(1)}, bf16[1,512,128]{2,1,0:T(8,128)(2,1)}, u32[]{:S(2)}) copy-start(bf16[1,512,128]{2,1,0:T(8,128)(2,1)} %param.7) | copy-start | bytes 393220
where the time goes:
time: 52.1 us; the launch traced here: 51.9 us
  Pallas kernels  44.4 us (85%)
  local copies, waits for them, and re-layouts  6.91 us (13%)
  between operations  0.65 us (1%)
    pallas_call x1, Pallas kernels, per_device(): pl.pallas_call(kernel, out_shape=[jax.ShapeDtypeStruct(flat, BF16)] * 3 +...  44.4 us
    unnamed x14, local copies, waits for them, and re-layouts  6.91 us

commit v1 on v0

v1 whole, which is shorter than its diff:
```python
import functools

import jax
import jax.numpy as jnp
from jax import lax
from jax.experimental import pallas as pl
from jax.experimental.pallas import tpu as pltpu
from jax.sharding import PartitionSpec as P

MESH = pl.DeviceIdType.MESH
F32 = jnp.float32
BF16 = jnp.bfloat16

PEERS = 64
NFL = 8
TOK = 128
LAGS = 32
SPAN = LAGS * TOK
PARTS = 2
QUAD = NFL // PARTS


def anti_identity(n, dtype):
    row = lax.broadcasted_iota(jnp.int32, (n, n), 0)
    col = lax.broadcasted_iota(jnp.int32, (n, n), 1)
    return (row + col == n - 1).astype(dtype)


def partner(k, seq):
    z, y, c = seq >> 3, (seq >> 1) & 3, seq & 1
    dz, dy, dc = (3 * k) & 7, ((k >> 3) + k) & 3, k >> 5
    return (((((z + dz) & 7) << 2) + ((y + dy) & 3)) << 1) + (c ^ dc)


def kernel(
    lengths_hbm, value_hbm, gate_hbm, cot_hbm, filt_hbm,
    gated, grad_value, grad_gate, grad_filters,
    lengths, value, gate, cot, filt,
    send1, recv1, send2, recv2, unpacked, result, xpad, gpad, toep, xcat, diag, sums, gsend, grecv,
    insem, ssem1, rsem1, ssem2, rsem2, gssem, grsem,
):
    seq = lax.axis_index("seq")
    ch = lax.axis_index("ch")

    loads = [
        pltpu.make_async_copy(src, dst, insem.at[n])
        for n, (src, dst) in enumerate(
            [(cot_hbm, cot), (gate_hbm, gate), (value_hbm, value),
             (filt_hbm.at[:, pl.ds(0, SPAN)], filt), (lengths_hbm, lengths)]
        )
    ]
    for load in loads:
        load.start()

    barrier = pltpu.get_barrier_semaphore()

    def greet(k, carry):
        pl.semaphore_signal(barrier, inc=1, device_id=(partner(k, seq), ch), device_id_type=MESH)
        return carry

    lax.fori_loop(1, PEERS, greet, 0, unroll=7)
    for step in range(1, 4):
        pl.semaphore_signal(barrier, inc=1, device_id=(seq, (ch + step) & 3), device_id_type=MESH)

    upper = lax.broadcasted_iota(jnp.int32, (PEERS, NFL, TOK), 1) < QUAD
    flip = anti_identity(TOK, BF16)
    for load in loads[:3]:
        load.wait()
    grad_conv = (cot[...].astype(F32) * gate[...].astype(F32)).astype(BF16)
    reverse = jnp.dot(grad_conv, flip, preferred_element_type=F32).reshape(PEERS, NFL, TOK)
    wide = value[...].astype(F32).reshape(PEERS, NFL, TOK)
    send1[0] = jnp.where(upper, wide, pltpu.roll(reverse, QUAD, 1)).astype(BF16)
    send1[1] = jnp.where(upper, pltpu.roll(wide, QUAD, 1), reverse).astype(BF16)

    def exchange(src, dst, ssem, rsem, part):
        def share(k, carry):
            to = partner(k, seq)
            pltpu.make_async_remote_copy(
                src_ref=src.at[part, to], dst_ref=dst.at[part, seq],
                send_sem=ssem.at[part], recv_sem=rsem.at[part],
                device_id=(to, ch), device_id_type=MESH,
            ).start()
            return carry

        lax.fori_loop(1, PEERS, share, 0, unroll=7)
        dst[part, pl.ds(seq, 1)] = src[part, pl.ds(seq, 1)]

    def finish(buffer, sem, part):
        blocks = buffer.at[part, pl.ds(0, PEERS - 1)]
        pltpu.make_async_copy(blocks, blocks, sem.at[part]).wait()

    pl.semaphore_wait(barrier, PEERS + 2)
    for part in range(PARTS):
        exchange(send1, recv1, ssem1, rsem1, part)

    loads[3].wait()
    loads[4].wait()
    lane_zero = jnp.zeros((8, TOK), F32)
    for f in range(NFL):
        row = jnp.broadcast_to(filt[f : f + 1, :], (8, SPAN))
        row = jnp.concatenate([lane_zero, row], axis=1)
        for q in range(0, 16, 2):
            top = pltpu.roll(row, 8 * q, 1, stride=1, stride_axis=0)
            low = pltpu.roll(row, 8 * q + 8, 1, stride=1, stride_axis=0)
            toep[f, 8 * q : 8 * q + 16, :] = jnp.concatenate([top, low], axis=0).astype(BF16)

    block = lax.broadcasted_iota(jnp.int32, (PEERS, TOK), 0)
    first = jnp.zeros((PEERS, TOK), jnp.int32)
    last = jnp.full((PEERS, TOK), PEERS, jnp.int32)
    edge = jnp.int32(0)
    for genome in range(4):
        first = jnp.where(block >= edge, edge, first)
        edge = edge + (lengths[genome] >> 7)
        last = jnp.minimum(last, jnp.where(block < edge, edge, PEERS))
    before = block - first
    after = last - 1 - block

    xpad[:, 0:LAGS, :] = jnp.zeros((NFL, LAGS, TOK), F32)
    gpad[:, PEERS : PEERS + LAGS, :] = jnp.zeros((NFL, LAGS, TOK), F32)

    def convolve(part):
        unpacked[part] = recv1[part].astype(F32).reshape(PEERS * 8, TOK)
        for e in range(QUAD):
            f = QUAD * part + e
            xpad[f, LAGS : LAGS + PEERS, :] = unpacked[part, pl.ds(e, PEERS, stride=8), :]
            gpad[f, 0:PEERS, :] = unpacked[part, pl.ds(QUAD + e, PEERS, stride=8), :]
            left, right = [], []
            for lag in range(LAGS):
                back = jnp.where(before >= lag, xpad[f, LAGS - lag : LAGS - lag + PEERS, :], 0.0)
                ahead = jnp.where(after >= lag, gpad[f, lag : lag + PEERS, :], 0.0)
                piece = jnp.concatenate([back, ahead], axis=0).astype(BF16)
                xcat[f, :, TOK * lag : TOK * lag + TOK] = piece[0:PEERS]
                left.append(piece)
                right.append(toep[f, :, TOK * lag + TOK : TOK * lag + 2 * TOK])
            out = jnp.dot(
                jnp.concatenate(left, axis=1), jnp.concatenate(right, axis=0),
                preferred_element_type=F32,
            )
            back = jnp.dot(out[PEERS:].astype(BF16), flip, preferred_element_type=F32)
            result[part, pl.ds(e, PEERS, stride=8), :] = out[0:PEERS]
            result[part, pl.ds(QUAD + e, PEERS, stride=8), :] = back
        send2[part] = result[part].reshape(PEERS, 8, TOK).astype(BF16)

    def correlate(part):
        for e in range(QUAD):
            f = QUAD * part + e
            lhs = gpad[f, 0:PEERS, :].T.astype(BF16)
            rhs = [xcat[f, :, TOK * lag : TOK * lag + TOK] for lag in range(LAGS - 1, -1, -1)]
            cross = jnp.dot(lhs, jnp.concatenate(rhs, axis=1), preferred_element_type=F32)
            cross = jnp.concatenate([cross, jnp.zeros((TOK, TOK), F32)], axis=1)
            skew = pltpu.roll(cross[0:8], 0, 1, stride=1, stride_axis=0)
            for q in range(1, 16):
                skew = skew + pltpu.roll(cross[8 * q : 8 * q + 8], 8 * q, 1, stride=1, stride_axis=0)
            for tile in range(LAGS):
                diag[f, 8 * tile : 8 * tile + 8, :] = skew[:, TOK * tile : TOK * tile + TOK]
            total = diag[f, pl.ds(0, LAGS, stride=8), :]
            for j in range(1, 8):
                total = total + diag[f, pl.ds(j, LAGS, stride=8), :]
            sums[LAGS * f : LAGS * f + LAGS, :] = total

    for part in range(PARTS):
        finish(recv1, rsem1, part)
        convolve(part)
        exchange(send2, recv2, ssem2, rsem2, part)
    for part in range(PARTS):
        correlate(part)

    totals = jnp.dot(
        sums[...], anti_identity(TOK, F32), precision=lax.Precision.HIGHEST, preferred_element_type=F32
    )
    for f in range(NFL):
        gsend[0, 16 * f : 16 * f + 16, :] = totals[LAGS * f + 16 : LAGS * f + 32]
        gsend[1, 16 * f : 16 * f + 16, :] = totals[LAGS * f : LAGS * f + 16]

    for part in range(2):
        copy = pltpu.make_async_remote_copy(
            src_ref=gsend.at[part], dst_ref=grecv.at[ch], send_sem=gssem.at[part], recv_sem=grsem.at[ch],
            device_id=(seq, jnp.int32(part)), device_id_type=MESH,
        )
        pl.when(ch != part)(copy.start)

        @pl.when(ch == part)
        def _():
            grecv[pl.ds(ch, 1)] = gsend[part : part + 1]

    for part in range(PARTS):
        finish(recv2, rsem2, part)
    early = recv2[0].astype(F32)
    late = recv2[1].astype(F32)
    conv = jnp.where(upper, early, pltpu.roll(late, QUAD, 1)).reshape(PEERS * NFL, TOK)
    back = jnp.where(upper, pltpu.roll(early, QUAD, 1), late).reshape(PEERS * NFL, TOK)
    gated[...] = (gate[...].astype(F32) * conv).astype(BF16)
    grad_gate[...] = (cot[...].astype(F32) * conv).astype(BF16)
    grad_value[...] = back.astype(BF16)

    for part in range(PARTS):
        finish(send1, ssem1, part)
        finish(send2, ssem2, part)
    for part in range(2):
        @pl.when(ch != part)
        def _():
            pltpu.make_async_copy(gsend.at[part], gsend.at[part], gssem.at[part]).wait()

    @pl.when(ch < 2)
    def _():
        for source in range(4):
            @pl.when(ch != source)
            def _():
                pltpu.make_async_copy(grecv.at[source], grecv.at[source], grsem.at[source]).wait()
        sums[0:128, :] = grecv[0] + grecv[1] + grecv[2] + grecv[3]
        for tile in range(16):
            grad_filters[:, TOK * (15 - tile) : TOK * (16 - tile)] = sums[pl.ds(tile, NFL, stride=16), :]

    @pl.when(ch >= 2)
    def _():
        grad_filters[...] = jnp.zeros((NFL, 2048), F32)


def per_device(value_in, gate_in, grad_out, filters, genome_lengths):
    shape = value_in.shape
    flat = (shape[1], shape[2])
    vmem = pl.BlockSpec(memory_space=pltpu.VMEM)
    hbm = pl.BlockSpec(memory_space=pl.ANY)
    messages = pltpu.VMEM((PARTS, PEERS, 8, TOK), BF16)
    outs = pl.pallas_call(
        kernel,
        out_shape=[jax.ShapeDtypeStruct(flat, BF16)] * 3 + [jax.ShapeDtypeStruct((NFL, 2048), F32)],
        in_specs=[hbm] * 5,
        out_specs=[vmem] * 4,
        scratch_shapes=[
            pltpu.SMEM((4,), jnp.int32),
            pltpu.VMEM(flat, BF16), pltpu.VMEM(flat, BF16), pltpu.VMEM(flat, BF16),
            pltpu.VMEM((NFL, SPAN), F32),
            messages, messages, messages, messages,
            pltpu.VMEM((PARTS, PEERS * 8, TOK), F32), pltpu.VMEM((PARTS, PEERS * 8, TOK), F32),
            pltpu.VMEM((NFL, PEERS + LAGS, TOK), F32), pltpu.VMEM((NFL, PEERS + LAGS, TOK), F32),
            pltpu.VMEM((NFL, TOK, SPAN + TOK), BF16),
            pltpu.VMEM((NFL, PEERS, SPAN), BF16),
            pltpu.VMEM((NFL, 8 * LAGS, TOK), F32), pltpu.VMEM((NFL * LAGS, TOK), F32),
            pltpu.VMEM((2, 128, TOK), F32), pltpu.VMEM((4, 128, TOK), F32),
            pltpu.SemaphoreType.DMA((5,)),
            pltpu.SemaphoreType.DMA((PARTS,)), pltpu.SemaphoreType.DMA((PARTS,)),
            pltpu.SemaphoreType.DMA((PARTS,)), pltpu.SemaphoreType.DMA((PARTS,)),
            pltpu.SemaphoreType.DMA((2,)), pltpu.SemaphoreType.DMA((4,)),
        ],
        compiler_params=pltpu.CompilerParams(
            collective_id=0, has_side_effects=True, vmem_limit_bytes=58 * 1024 * 1024
        ),
        name="hyena",
    )(genome_lengths, value_in.reshape(flat), gate_in.reshape(flat), grad_out.reshape(flat), filters)
    return (outs[0].reshape(shape), outs[1].reshape(shape), outs[2].reshape(shape), outs[3])


def solution(mesh):
    tokens = P("ch", None, "seq")
    return jax.shard_map(
        per_device,
        mesh=mesh,
        in_specs=(tokens, tokens, tokens, P("seq", None), P()),
        out_specs=(tokens, tokens, tokens, P("seq", "ch")),
        check_vma=False,
    )
```

time: 52.1 us -> 40.7 us (0.78)
  Pallas kernels: 44.4 us -> 35.8 us
  local copies, waits for them, and re-layouts: 6.91 us -> 4.05 us
    pallas_call x1, Pallas kernels: 44.4 us -> 35.8 us  [per_device(): pl.pallas_call(kernel, out_shape=[jax.ShapeDtypeStruct(flat, BF16)] * 3 +...]
    unnamed x14 -> x10, local copies, waits for them, and re-layouts: 6.91 us -> 4.05 us
where the time goes in v1:
time: 40.7 us; the launch traced here: 40.5 us
  Pallas kernels  35.8 us (88%)
  local copies, waits for them, and re-layouts  4.05 us (10%)
  between operations  0.65 us (2%)
    pallas_call x1, Pallas kernels, per_device(): pl.pallas_call(kernel, out_shape=[jax.ShapeDtypeStruct(flat, BF16)] * 3 +...  35.8 us
    unnamed x10, local copies, waits for them, and re-layouts  4.05 us

profile of v1, /device:TPU:1, one launch (start us, length us, event | category | flops | bytes accessed | tf_op | source)
XLA Modules:
  0.0 40.5 jit_solution(17112072523247133712)
XLA Ops:
  0.6 35.8 %hyena.1 = (bf16[512,128]{1,0:T(8,128)(2,1)}, bf16[512,128]{1,0:T(8,128)(2,1)}, bf16[512,128]{1,0:T(8,128)(2,1)}, f32[8,2048]{1,0:T(8,128)}) custom-call(s32[4]{0:T(128)} %lengths_hbm.1, bf16[512,128]{1,0:T(8,128)(2,1)} %bitcast.9, bf16[512,128]{1,0:T(8,128)(2,1)} %bitcast.10, bf16[512,128]{1,0:T(8,128)(2,1)} %bitcast.11, f32[8,8192]{1,0:T(8,128)} %filt_hbm.1), custom_call_target="tpu_custom_call" | custom-call | tf_op jit(solution)/shard_map/hyena/pallas_call | solution.py:225
  36.5 0.0 copy-start.1
  36.5 1.6 %copy.13 = bf16[1,512,128]{2,1,0:T(8,128)(2,1)} copy(bf16[1,512,128]{2,1,0:T(8,128)(2,1)} %bitcast.8) | data formatting | bytes 262144
  38.1 0.0 copy-done.1
  38.1 0.0 copy-start
  38.1 0.7 %copy.14 = bf16[1,512,128]{2,1,0:T(8,128)(2,1)} copy(bf16[1,512,128]{2,1,0:T(8,128)(2,1)S(1)} %bitcast.7) | data formatting | bytes 262144
  38.7 0.3 copy-done
  39.0 0.0 copy-start.2
  39.0 0.7 %copy.15 = bf16[1,512,128]{2,1,0:T(8,128)(2,1)} copy(bf16[1,512,128]{2,1,0:T(8,128)(2,1)S(1)} %bitcast.6) | data formatting | bytes 262144
  39.7 0.2 copy-done.2
  39.9 0.6 %copy.16 = f32[8,2048]{1,0:T(8,128)} copy(f32[8,2048]{1,0:T(8,128)S(1)} %copy-done.2) | data formatting | bytes 131072
Async XLA Ops:
  36.5 1.6 %copy-start.1 = (bf16[512,128]{1,0:T(8,128)(2,1)S(1)}, bf16[512,128]{1,0:T(8,128)(2,1)}, u32[]{:S(2)}) copy-start(bf16[512,128]{1,0:T(8,128)(2,1)} %get-tuple-element.9) | copy-start | bytes 393220
  38.1 1.0 %copy-start = (bf16[512,128]{1,0:T(8,128)(2,1)S(1)}, bf16[512,128]{1,0:T(8,128)(2,1)}, u32[]{:S(2)}) copy-start(bf16[512,128]{1,0:T(8,128)(2,1)} %get-tuple-element.10) | copy-start | bytes 393220
  39.0 0.9 %copy-start.2 = (f32[8,2048]{1,0:T(8,128)S(1)}, f32[8,2048]{1,0:T(8,128)}, u32[]{:S(2)}) copy-start(f32[8,2048]{1,0:T(8,128)} %get-tuple-element.19) | copy-start | bytes 196612

commit v2 on v1

--- a/solution.py
+++ b/solution.py
@@ -34,10 +34,10 @@
 
 def kernel(
     lengths_hbm, value_hbm, gate_hbm, cot_hbm, filt_hbm,
-    gated, grad_value, grad_gate, grad_filters,
-    lengths, value, gate, cot, filt,
-    send1, recv1, send2, recv2, unpacked, result, xpad, gpad, toep, xcat, diag, sums, gsend, grecv,
-    insem, ssem1, rsem1, ssem2, rsem2, gssem, grsem,
+    recv2, gate, cot, grad_filters,
+    lengths, value, filt,
+    send1, recv1, send2, unpacked, result, xpad, gpad, toep, xcat, diag, sums, gsend, grecv,
+    insem, ssem1, rsem1, ssem2, rsem2, gssem, grsem, ownsem,
 ):
     seq = lax.axis_index("seq")
     ch = lax.axis_index("ch")
@@ -83,15 +83,16 @@
             return carry
 
         lax.fori_loop(1, PEERS, share, 0, unroll=7)
-        dst[part, pl.ds(seq, 1)] = src[part, pl.ds(seq, 1)]
+        own = pltpu.make_async_copy(src.at[part, seq], dst.at[part, seq], ownsem.at[part])
+        own.start()
+        return own
 
     def finish(buffer, sem, part):
         blocks = buffer.at[part, pl.ds(0, PEERS - 1)]
         pltpu.make_async_copy(blocks, blocks, sem.at[part]).wait()
 
     pl.semaphore_wait(barrier, PEERS + 2)
-    for part in range(PARTS):
-        exchange(send1, recv1, ssem1, rsem1, part)
+    own1 = [exchange(send1, recv1, ssem1, rsem1, part) for part in range(PARTS)]
 
     loads[3].wait()
     loads[4].wait()
@@ -158,56 +159,46 @@
                 total = total + diag[f, pl.ds(j, LAGS, stride=8), :]
             sums[LAGS * f : LAGS * f + LAGS, :] = total
 
+    def collect(half):
+        totals = jnp.dot(
+            sums[LAGS * QUAD * half : LAGS * QUAD * (half + 1), :], anti_identity(TOK, F32),
+            precision=lax.Precision.HIGHEST, preferred_element_type=F32,
+        )
+        for e in range(QUAD):
+            gsend[half, 0, 16 * e : 16 * e + 16, :] = totals[LAGS * e + 16 : LAGS * e + 32]
+            gsend[half, 1, 16 * e : 16 * e + 16, :] = totals[LAGS * e : LAGS * e + 16]
+        for to in range(2):
+            copy = pltpu.make_async_remote_copy(
+                src_ref=gsend.at[half, to], dst_ref=grecv.at[half, ch],
+                send_sem=gssem.at[half, to], recv_sem=grsem.at[half, ch],
+                device_id=(seq, jnp.int32(to)), device_id_type=MESH,
+            )
+            pl.when(ch != to)(copy.start)
+
+            @pl.when(ch == to)
+            def _():
+                grecv[half, pl.ds(ch, 1)] = gsend[half, to : to + 1]
+
+    own2 = []
     for part in range(PARTS):
         finish(recv1, rsem1, part)
+        own1[part].wait()
         convolve(part)
-        exchange(send2, recv2, ssem2, rsem2, part)
-    for part in range(PARTS):
+        own2.append(exchange(send2, recv2, ssem2, rsem2, part))
         correlate(part)
-
-    totals = jnp.dot(
-        sums[...], anti_identity(TOK, F32), precision=lax.Precision.HIGHEST, preferred_element_type=F32
-    )
-    for f in range(NFL):
-        gsend[0, 16 * f : 16 * f + 16, :] = totals[LAGS * f + 16 : LAGS * f + 32]
-        gsend[1, 16 * f : 16 * f + 16, :] = totals[LAGS * f : LAGS * f + 16]
-
-    for part in range(2):
-        copy = pltpu.make_async_remote_copy(
-            src_ref=gsend.at[part], dst_ref=grecv.at[ch], send_sem=gssem.at[part], recv_sem=grsem.at[ch],
-            device_id=(seq, jnp.int32(part)), device_id_type=MESH,
-        )
-        pl.when(ch != part)(copy.start)
-
-        @pl.when(ch == part)
-        def _():
-            grecv[pl.ds(ch, 1)] = gsend[part : part + 1]
-
-    for part in range(PARTS):
-        finish(recv2, rsem2, part)
-    early = recv2[0].astype(F32)
-    late = recv2[1].astype(F32)
-    conv = jnp.where(upper, early, pltpu.roll(late, QUAD, 1)).reshape(PEERS * NFL, TOK)
-    back = jnp.where(upper, pltpu.roll(early, QUAD, 1), late).reshape(PEERS * NFL, TOK)
-    gated[...] = (gate[...].astype(F32) * conv).astype(BF16)
-    grad_gate[...] = (cot[...].astype(F32) * conv).astype(BF16)
-    grad_value[...] = back.astype(BF16)
-
-    for part in range(PARTS):
-        finish(send1, ssem1, part)
-        finish(send2, ssem2, part)
-    for part in range(2):
-        @pl.when(ch != part)
-        def _():
-            pltpu.make_async_copy(gsend.at[part], gsend.at[part], gssem.at[part]).wait()
+        collect(part)
 
     @pl.when(ch < 2)
     def _():
-        for source in range(4):
-            @pl.when(ch != source)
-            def _():
-                pltpu.make_async_copy(grecv.at[source], grecv.at[source], grsem.at[source]).wait()
-        sums[0:128, :] = grecv[0] + grecv[1] + grecv[2] + grecv[3]
+        for half in range(PARTS):
+            for source in range(4):
+                @pl.when(ch != source)
+                def _():
+                    piece = grecv.at[half, source]
+                    pltpu.make_async_copy(piece, piece, grsem.at[half, source]).wait()
+            sums[64 * half : 64 * half + 64, :] = (
+                grecv[half, 0] + grecv[half, 1] + grecv[half, 2] + grecv[half, 3]
+            )
         for tile in range(16):
             grad_filters[:, TOK * (15 - tile) : TOK * (16 - tile)] = sums[pl.ds(tile, NFL, stride=16), :]
 
@@ -215,39 +206,90 @@
     def _():
         grad_filters[...] = jnp.zeros((NFL, 2048), F32)
 
+    for part in range(PARTS):
+        finish(recv2, rsem2, part)
+        own2[part].wait()
+        finish(send1, ssem1, part)
+        finish(send2, ssem2, part)
+        for to in range(2):
+            @pl.when(ch != to)
+            def _():
+                piece = gsend.at[part, to]
+                pltpu.make_async_copy(piece, piece, gssem.at[part, to]).wait()
+
+
+def gating(recv2, gate, cot, part_filters, gated, grad_value, grad_gate, grad_filters, out1, out2, out3, sem):
+    filters = pltpu.make_async_copy(part_filters, grad_filters, sem.at[3])
+    filters.start()
+    upper = lax.broadcasted_iota(jnp.int32, (PEERS, NFL, TOK), 1) < QUAD
+    early = recv2[0].astype(F32)
+    late = recv2[1].astype(F32)
+    back = jnp.where(upper, pltpu.roll(early, QUAD, 1), late).reshape(PEERS * NFL, TOK)
+    out1[...] = back.astype(BF16)
+    store1 = pltpu.make_async_copy(out1, grad_value, sem.at[0])
+    store1.start()
+    conv = jnp.where(upper, early, pltpu.roll(late, QUAD, 1)).reshape(PEERS * NFL, TOK)
+    out2[...] = (gate[...].astype(F32) * conv).astype(BF16)
+    store2 = pltpu.make_async_copy(out2, gated, sem.at[1])
+    store2.start()
+    out3[...] = (cot[...].astype(F32) * conv).astype(BF16)
+    store3 = pltpu.make_async_copy(out3, grad_gate, sem.at[2])
+    store3.start()
+    for store in (filters, store1, store2, store3):
+        store.wait()
+
 
 def per_device(value_in, gate_in, grad_out, filters, genome_lengths):
     shape = value_in.shape
     flat = (shape[1], shape[2])
+    hbm = pl.BlockSpec(memory_space=pltpu.HBM)
+    messages = pltpu.VMEM((PARTS, PEERS, 8, TOK), BF16)
+    flats = [array.reshape(flat) for array in (value_in, gate_in, grad_out)]
+    tail = jax.ShapeDtypeStruct((NFL, 2048), F32)
     vmem = pl.BlockSpec(memory_space=pltpu.VMEM)
-    hbm = pl.BlockSpec(memory_space=pl.ANY)
-    messages = pltpu.VMEM((PARTS, PEERS, 8, TOK), BF16)
+    held = [
+        pltpu.with_memory_space_constraint(array, pltpu.HBM)
+        for array in (genome_lengths, *flats, filters)
+    ]
     outs = pl.pallas_call(
         kernel,
-        out_shape=[jax.ShapeDtypeStruct(flat, BF16)] * 3 + [jax.ShapeDtypeStruct((NFL, 2048), F32)],
+        out_shape=[
+            jax.ShapeDtypeStruct((PARTS, PEERS, 8, TOK), BF16),
+            jax.ShapeDtypeStruct(flat, BF16), jax.ShapeDtypeStruct(flat, BF16), tail,
+        ],
         in_specs=[hbm] * 5,
         out_specs=[vmem] * 4,
         scratch_shapes=[
             pltpu.SMEM((4,), jnp.int32),
-            pltpu.VMEM(flat, BF16), pltpu.VMEM(flat, BF16), pltpu.VMEM(flat, BF16),
+            pltpu.VMEM(flat, BF16),
             pltpu.VMEM((NFL, SPAN), F32),
-            messages, messages, messages, messages,
+            messages, messages, messages,
             pltpu.VMEM((PARTS, PEERS * 8, TOK), F32), pltpu.VMEM((PARTS, PEERS * 8, TOK), F32),
             pltpu.VMEM((NFL, PEERS + LAGS, TOK), F32), pltpu.VMEM((NFL, PEERS + LAGS, TOK), F32),
             pltpu.VMEM((NFL, TOK, SPAN + TOK), BF16),
             pltpu.VMEM((NFL, PEERS, SPAN), BF16),
             pltpu.VMEM((NFL, 8 * LAGS, TOK), F32), pltpu.VMEM((NFL * LAGS, TOK), F32),
-            pltpu.VMEM((2, 128, TOK), F32), pltpu.VMEM((4, 128, TOK), F32),
+            pltpu.VMEM((PARTS, 2, 64, TOK), F32), pltpu.VMEM((PARTS, 4, 64, TOK), F32),
             pltpu.SemaphoreType.DMA((5,)),
             pltpu.SemaphoreType.DMA((PARTS,)), pltpu.SemaphoreType.DMA((PARTS,)),
             pltpu.SemaphoreType.DMA((PARTS,)), pltpu.SemaphoreType.DMA((PARTS,)),
-            pltpu.SemaphoreType.DMA((2,)), pltpu.SemaphoreType.DMA((4,)),
+            pltpu.SemaphoreType.DMA((PARTS, 2)), pltpu.SemaphoreType.DMA((PARTS, 4)),
+            pltpu.SemaphoreType.DMA((PARTS,)),
         ],
         compiler_params=pltpu.CompilerParams(
-            collective_id=0, has_side_effects=True, vmem_limit_bytes=58 * 1024 * 1024
+            collective_id=0, has_side_effects=True, vmem_limit_bytes=40 * 1024 * 1024
         ),
         name="hyena",
-    )(genome_lengths, value_in.reshape(flat), gate_in.reshape(flat), grad_out.reshape(flat), filters)
+    )(*held)
+    outs = pl.pallas_call(
+        gating,
+        out_shape=[jax.ShapeDtypeStruct(flat, BF16)] * 3 + [tail],
+        in_specs=[vmem] * 4,
+        out_specs=[hbm] * 4,
+        scratch_shapes=[pltpu.VMEM(flat, BF16)] * 3 + [pltpu.SemaphoreType.DMA((4,))],
+        compiler_params=pltpu.CompilerParams(vmem_limit_bytes=8 * 1024 * 1024),
+        name="gating",
+    )(*outs)
     return (outs[0].reshape(shape), outs[1].reshape(shape), outs[2].reshape(shape), outs[3])
 
 

time: 40.7 us -> 35.5 us (0.87)
  local copies, waits for them, and re-layouts: 4.05 us -> 0 us
  Pallas kernels: 35.8 us -> 34.8 us
    unnamed x10 -> x0, local copies, waits for them, and re-layouts: 4.05 us -> none
    pallas_call x1 -> x2, Pallas kernels: 35.8 us -> 34.8 us  [the longest x1 33.9 us: per_device(): pl.pallas_call(kernel, out_shape=[jax.ShapeDtypeStruct((PARTS, PEERS, 8,...]
where the time goes in v2:
time: 35.5 us; the launch traced here: 35.4 us
  Pallas kernels  34.8 us (98%)
  between operations  0.64 us (2%)
    pallas_call x1, Pallas kernels, per_device(): pl.pallas_call(kernel, out_shape=[jax.ShapeDtypeStruct((PARTS, PEERS, 8,...  33.9 us
    pallas_call x1, Pallas kernels, per_device(): pl.pallas_call(gating, out_shape=[jax.ShapeDtypeStruct(flat, BF16)] * 3 +...  0.83 us

profile of v2, /device:TPU:1, one launch (start us, length us, event | category | flops | bytes accessed | tf_op | source)
XLA Modules:
  0.0 35.4 jit_solution(10298677419961920409)
XLA Ops:
  0.6 33.9 %hyena.1 = (bf16[2,64,8,128]{3,2,1,0:T(8,128)(2,1)S(1)}, bf16[512,128]{1,0:T(8,128)(2,1)S(1)}, bf16[512,128]{1,0:T(8,128)(2,1)S(1)}, f32[8,2048]{1,0:T(8,128)S(1)}) custom-call(s32[4]{0:T(128)} %lengths_hbm.1, bf16[512,128]{1,0:T(8,128)(2,1)} %bitcast.6, bf16[512,128]{1,0:T(8,128)(2,1)} %bitcast.7, bf16[512,128]{1,0:T(8,128)(2,1)} %bitcast.8, f32[8,8192]{1,0:T(8,128)} %filt_hbm.1), custom_call_target="tpu_custom_call" | custom-call | tf_op jit(solution)/shard_map/hyena/pallas_call | solution.py:254
  34.6 0.8 %gating.1 = (bf16[512,128]{1,0:T(8,128)(2,1)}, bf16[512,128]{1,0:T(8,128)(2,1)}, bf16[512,128]{1,0:T(8,128)(2,1)}, f32[8,2048]{1,0:T(8,128)}) custom-call(bf16[2,64,8,128]{3,2,1,0:T(8,128)(2,1)S(1)} %get-tuple-element.12.recv2, bf16[512,128]{1,0:T(8,128)(2,1)S(1)} %get-tuple-element.13.gate, bf16[512,128]{1,0:T(8,128)(2,1)S(1)} %get-tuple-element.14.cot, ...), custom_call_target="tpu_custom_call" | custom-call | tf_op jit(solution)/shard_map/gating/pallas_call | solution.py:284

commit v3 on v2

--- a/solution.py
+++ b/solution.py
@@ -28,7 +28,10 @@
 
 def partner(k, seq):
     z, y, c = seq >> 3, (seq >> 1) & 3, seq & 1
-    dz, dy, dc = (3 * k) & 7, ((k >> 3) + k) & 3, k >> 5
+    k = (PEERS - k) & (PEERS - 1)
+    near = (k >> 3) + 1
+    dz = ((near >> 1) * (1 - 2 * (near & 1))) & 7
+    dy, dc = (k >> 1) & 3, k & 1
     return (((((z + dz) & 7) << 2) + ((y + dy) & 3)) << 1) + (c ^ dc)
 
 
@@ -121,6 +124,7 @@
 
     def convolve(part):
         unpacked[part] = recv1[part].astype(F32).reshape(PEERS * 8, TOK)
+        backs = []
         for e in range(QUAD):
             f = QUAD * part + e
             xpad[f, LAGS : LAGS + PEERS, :] = unpacked[part, pl.ds(e, PEERS, stride=8), :]
@@ -137,9 +141,11 @@
                 jnp.concatenate(left, axis=1), jnp.concatenate(right, axis=0),
                 preferred_element_type=F32,
             )
-            back = jnp.dot(out[PEERS:].astype(BF16), flip, preferred_element_type=F32)
             result[part, pl.ds(e, PEERS, stride=8), :] = out[0:PEERS]
-            result[part, pl.ds(QUAD + e, PEERS, stride=8), :] = back
+            backs.append(out[PEERS:].astype(BF16))
+        back = jnp.dot(jnp.concatenate(backs, axis=0), flip, preferred_element_type=F32)
+        for e in range(QUAD):
+            result[part, pl.ds(QUAD + e, PEERS, stride=8), :] = back[PEERS * e : PEERS * e + PEERS]
         send2[part] = result[part].reshape(PEERS, 8, TOK).astype(BF16)
 
     def correlate(part):
@@ -160,13 +166,10 @@
             sums[LAGS * f : LAGS * f + LAGS, :] = total
 
     def collect(half):
-        totals = jnp.dot(
-            sums[LAGS * QUAD * half : LAGS * QUAD * (half + 1), :], anti_identity(TOK, F32),
-            precision=lax.Precision.HIGHEST, preferred_element_type=F32,
-        )
         for e in range(QUAD):
-            gsend[half, 0, 16 * e : 16 * e + 16, :] = totals[LAGS * e + 16 : LAGS * e + 32]
-            gsend[half, 1, 16 * e : 16 * e + 16, :] = totals[LAGS * e : LAGS * e + 16]
+            f = QUAD * half + e
+            gsend[half, 0, 16 * e : 16 * e + 16, :] = sums[LAGS * f + 16 : LAGS * f + 32]
+            gsend[half, 1, 16 * e : 16 * e + 16, :] = sums[LAGS * f : LAGS * f + 16]
         for to in range(2):
             copy = pltpu.make_async_remote_copy(
                 src_ref=gsend.at[half, to], dst_ref=grecv.at[half, ch],
@@ -196,8 +199,10 @@
                 def _():
                     piece = grecv.at[half, source]
                     pltpu.make_async_copy(piece, piece, grsem.at[half, source]).wait()
-            sums[64 * half : 64 * half + 64, :] = (
-                grecv[half, 0] + grecv[half, 1] + grecv[half, 2] + grecv[half, 3]
+            sums[64 * half : 64 * half + 64, :] = jnp.dot(
+                grecv[half, 0] + grecv[half, 1] + grecv[half, 2] + grecv[half, 3],
+                anti_identity(TOK, F32),
+                precision=lax.Precision.HIGHEST, preferred_element_type=F32,
             )
         for tile in range(16):
             grad_filters[:, TOK * (15 - tile) : TOK * (16 - tile)] = sums[pl.ds(tile, NFL, stride=16), :]

time: 35.5 us -> 34 us (0.958)
  Pallas kernels: 34.8 us -> 33.3 us
    pallas_call x1, Pallas kernels: 33.9 us -> 32.4 us  [per_device(): pl.pallas_call(kernel, out_shape=[jax.ShapeDtypeStruct((PARTS, PEERS, 8,...]
where the time goes in v3:
time: 34 us; the launch traced here: 33.9 us
  Pallas kernels  33.3 us (98%)
  between operations  0.64 us (2%)
    pallas_call x1, Pallas kernels, per_device(): pl.pallas_call(kernel, out_shape=[jax.ShapeDtypeStruct((PARTS, PEERS, 8,...  32.4 us
    pallas_call x1, Pallas kernels, per_device(): pl.pallas_call(gating, out_shape=[jax.ShapeDtypeStruct(flat, BF16)] * 3 +...  0.83 us

profile of v3, /device:TPU:1, one launch (start us, length us, event | category | flops | bytes accessed | tf_op | source)
XLA Modules:
  0.0 33.9 jit_solution(8752809895428359406)
XLA Ops:
  0.6 32.4 %hyena.1 = (bf16[2,64,8,128]{3,2,1,0:T(8,128)(2,1)S(1)}, bf16[512,128]{1,0:T(8,128)(2,1)S(1)}, bf16[512,128]{1,0:T(8,128)(2,1)S(1)}, f32[8,2048]{1,0:T(8,128)S(1)}) custom-call(s32[4]{0:T(128)} %lengths_hbm.1, bf16[512,128]{1,0:T(8,128)(2,1)} %bitcast.6, bf16[512,128]{1,0:T(8,128)(2,1)} %bitcast.7, bf16[512,128]{1,0:T(8,128)(2,1)} %bitcast.8, f32[8,8192]{1,0:T(8,128)} %filt_hbm.1), custom_call_target="tpu_custom_call" | custom-call | tf_op jit(solution)/shard_map/hyena/pallas_call | solution.py:259
  33.1 0.8 %gating.1 = (bf16[512,128]{1,0:T(8,128)(2,1)}, bf16[512,128]{1,0:T(8,128)(2,1)}, bf16[512,128]{1,0:T(8,128)(2,1)}, f32[8,2048]{1,0:T(8,128)}) custom-call(bf16[2,64,8,128]{3,2,1,0:T(8,128)(2,1)S(1)} %get-tuple-element.12.recv2, bf16[512,128]{1,0:T(8,128)(2,1)S(1)} %get-tuple-element.13.gate, bf16[512,128]{1,0:T(8,128)(2,1)S(1)} %get-tuple-element.14.cot, ...), custom_call_target="tpu_custom_call" | custom-call | tf_op jit(solution)/shard_map/gating/pallas_call | solution.py:289

commit v4 on v3

--- a/solution.py
+++ b/solution.py
@@ -188,6 +188,7 @@
         own1[part].wait()
         convolve(part)
         own2.append(exchange(send2, recv2, ssem2, rsem2, part))
+    for part in range(PARTS):
         correlate(part)
         collect(part)
 

time: 34 us -> 33.8 us (level)
  no operation moved by 1% of the time
where the time goes in v4:
time: 33.8 us; the launch traced here: 33.7 us
  Pallas kernels  33.1 us (98%)
  between operations  0.64 us (2%)
    pallas_call x1, Pallas kernels, per_device(): pl.pallas_call(kernel, out_shape=[jax.ShapeDtypeStruct((PARTS, PEERS, 8,...  32.2 us
    pallas_call x1, Pallas kernels, per_device(): pl.pallas_call(gating, out_shape=[jax.ShapeDtypeStruct(flat, BF16)] * 3 +...  0.83 us

profile of v4, /device:TPU:1, one launch (start us, length us, event | category | flops | bytes accessed | tf_op | source)
XLA Modules:
  0.0 33.7 jit_solution(5616541082547562385)
XLA Ops:
  0.6 32.2 %hyena.1 = (bf16[2,64,8,128]{3,2,1,0:T(8,128)(2,1)S(1)}, bf16[512,128]{1,0:T(8,128)(2,1)S(1)}, bf16[512,128]{1,0:T(8,128)(2,1)S(1)}, f32[8,2048]{1,0:T(8,128)S(1)}) custom-call(s32[4]{0:T(128)} %lengths_hbm.1, bf16[512,128]{1,0:T(8,128)(2,1)} %bitcast.6, bf16[512,128]{1,0:T(8,128)(2,1)} %bitcast.7, bf16[512,128]{1,0:T(8,128)(2,1)} %bitcast.8, f32[8,8192]{1,0:T(8,128)} %filt_hbm.1), custom_call_target="tpu_custom_call" | custom-call | tf_op jit(solution)/shard_map/hyena/pallas_call | solution.py:260
  32.9 0.8 %gating.1 = (bf16[512,128]{1,0:T(8,128)(2,1)}, bf16[512,128]{1,0:T(8,128)(2,1)}, bf16[512,128]{1,0:T(8,128)(2,1)}, f32[8,2048]{1,0:T(8,128)}) custom-call(bf16[2,64,8,128]{3,2,1,0:T(8,128)(2,1)S(1)} %get-tuple-element.12.recv2, bf16[512,128]{1,0:T(8,128)(2,1)S(1)} %get-tuple-element.13.gate, bf16[512,128]{1,0:T(8,128)(2,1)S(1)} %get-tuple-element.14.cot, ...), custom_call_target="tpu_custom_call" | custom-call | tf_op jit(solution)/shard_map/gating/pallas_call | solution.py:290

commit v5 on v4

--- a/solution.py
+++ b/solution.py
@@ -168,8 +168,8 @@
     def collect(half):
         for e in range(QUAD):
             f = QUAD * half + e
-            gsend[half, 0, 16 * e : 16 * e + 16, :] = sums[LAGS * f + 16 : LAGS * f + 32]
-            gsend[half, 1, 16 * e : 16 * e + 16, :] = sums[LAGS * f : LAGS * f + 16]
+            gsend[half, 0, 16 * e : 16 * e + 16, :] = sums[LAGS * f + 16 : LAGS * f + 32].astype(BF16)
+            gsend[half, 1, 16 * e : 16 * e + 16, :] = sums[LAGS * f : LAGS * f + 16].astype(BF16)
         for to in range(2):
             copy = pltpu.make_async_remote_copy(
                 src_ref=gsend.at[half, to], dst_ref=grecv.at[half, ch],
@@ -201,7 +201,7 @@
                     piece = grecv.at[half, source]
                     pltpu.make_async_copy(piece, piece, grsem.at[half, source]).wait()
             sums[64 * half : 64 * half + 64, :] = jnp.dot(
-                grecv[half, 0] + grecv[half, 1] + grecv[half, 2] + grecv[half, 3],
+                jnp.sum(grecv[half].astype(F32), axis=0),
                 anti_identity(TOK, F32),
                 precision=lax.Precision.HIGHEST, preferred_element_type=F32,
             )
@@ -275,7 +275,7 @@
             pltpu.VMEM((NFL, TOK, SPAN + TOK), BF16),
             pltpu.VMEM((NFL, PEERS, SPAN), BF16),
             pltpu.VMEM((NFL, 8 * LAGS, TOK), F32), pltpu.VMEM((NFL * LAGS, TOK), F32),
-            pltpu.VMEM((PARTS, 2, 64, TOK), F32), pltpu.VMEM((PARTS, 4, 64, TOK), F32),
+            pltpu.VMEM((PARTS, 2, 64, TOK), BF16), pltpu.VMEM((PARTS, 4, 64, TOK), BF16),
             pltpu.SemaphoreType.DMA((5,)),
             pltpu.SemaphoreType.DMA((PARTS,)), pltpu.SemaphoreType.DMA((PARTS,)),
             pltpu.SemaphoreType.DMA((PARTS,)), pltpu.SemaphoreType.DMA((PARTS,)),

time: 33.8 us -> 33.5 us (level)
  no operation moved by 1% of the time
where the time goes in v5:
time: 33.5 us
  Pallas kernels  32.8 us (98%)
  between operations  0.64 us (2%)
    pallas_call x1, Pallas kernels, per_device(): pl.pallas_call(kernel, out_shape=[jax.ShapeDtypeStruct((PARTS, PEERS, 8,...  32 us
    pallas_call x1, Pallas kernels, per_device(): pl.pallas_call(gating, out_shape=[jax.ShapeDtypeStruct(flat, BF16)] * 3 +...  0.83 us

profile of v5, /device:TPU:1, one launch (start us, length us, event | category | flops | bytes accessed | tf_op | source)
XLA Modules:
  0.0 33.5 jit_solution(4094480380112283601)
XLA Ops:
  0.6 32.0 %hyena.1 = (bf16[2,64,8,128]{3,2,1,0:T(8,128)(2,1)S(1)}, bf16[512,128]{1,0:T(8,128)(2,1)S(1)}, bf16[512,128]{1,0:T(8,128)(2,1)S(1)}, f32[8,2048]{1,0:T(8,128)S(1)}) custom-call(s32[4]{0:T(128)} %lengths_hbm.1, bf16[512,128]{1,0:T(8,128)(2,1)} %bitcast.6, bf16[512,128]{1,0:T(8,128)(2,1)} %bitcast.7, bf16[512,128]{1,0:T(8,128)(2,1)} %bitcast.8, f32[8,8192]{1,0:T(8,128)} %filt_hbm.1), custom_call_target="tpu_custom_call" | custom-call | tf_op jit(solution)/shard_map/hyena/pallas_call | solution.py:260
  32.6 0.8 %gating.1 = (bf16[512,128]{1,0:T(8,128)(2,1)}, bf16[512,128]{1,0:T(8,128)(2,1)}, bf16[512,128]{1,0:T(8,128)(2,1)}, f32[8,2048]{1,0:T(8,128)}) custom-call(bf16[2,64,8,128]{3,2,1,0:T(8,128)(2,1)S(1)} %get-tuple-element.12.recv2, bf16[512,128]{1,0:T(8,128)(2,1)S(1)} %get-tuple-element.13.gate, bf16[512,128]{1,0:T(8,128)(2,1)S(1)} %get-tuple-element.14.cot, ...), custom_call_target="tpu_custom_call" | custom-call | tf_op jit(solution)/shard_map/gating/pallas_call | solution.py:290
